TPU v7x, 32 devices: a whole 2x2x4 slice. The times are simulated.
32 devices in a mesh: chan: 8 (over z, x), stn: 4 (over y, core).
Axes of the slice: x: 2, y: 2, z: 4, core: 2. Of those that a mesh axis runs over, the one named last changes fastest.
Arguments:
- gains: float32 [16, 2, 2, 2, 16, 512], P('chan', None, None, None, None, 'stn'), may hold values from -2.1 to 2.1
- coherency: bfloat16 [16, 16, 2, 512, 512], P('chan', None, None, 'stn'), may hold values from -1.5 to 1.5
- vis_data: bfloat16 [16, 2, 2, 2, 512, 512], P('chan', None, None, None, 'stn'), may hold values from -6 to 6
- flags: int32 [16, 32, 32], P('chan', 'stn'), may hold values 0 or 1
- beam: float32 [8, 16], replicated, may hold values from 0.5 to 2
- group_of: int32 [512], replicated, may hold values from 0 to 7
Outputs:
- gain_step: float32 [16, 2, 2, 2, 16, 512], P('chan', None, None, None, None, 'stn')
- loss_value: float32 [], replicated
All inputs are finite; a program needn't handle non-finite values. No bound on the sum of `flags` on one device may be relied on, other than what follows from the above.
Results may differ from a plain program's by a relative error of at most 0.0003.
Values sent between devices are 32-bit elements; how exact they have to be, the bound alone decides.
A program may use at most 128 MiB of HBM per device.

v0:
```python
import jax
import jax.numpy as jnp
from jax import lax
from jax.sharding import PartitionSpec as P

BLK = 16


smooth_weight = 0.05
damping = 0.3


def padded(cells, sides, width):
    for axis, dim in sides:
        count = lax.axis_size(axis)
        ends = count - 1
        head = lax.slice_in_dim(cells, 0, width, axis=dim)
        tail = lax.slice_in_dim(cells, cells.shape[dim] - width, cells.shape[dim], axis=dim)
        cells = jnp.concatenate(
            [
                lax.ppermute(tail, axis, [(i, (i + 1) % count) for i in range(ends)]),
                cells,
                lax.ppermute(head, axis, [((i + 1) % count, i) for i in range(ends)]),
            ],
            axis=dim,
        )
    return cells


def beam_factor(beam, group_of):
    groups = beam.shape[0]
    onehot = (group_of[None, :] == jnp.arange(groups, dtype=jnp.int32)[:, None]).astype(jnp.float32)
    return jnp.sum(beam[:, :, None] * onehot[:, None, :], axis=0)


def expand_flags(flags):
    chans, first, second = flags.shape
    wide = jnp.broadcast_to(
        flags.astype(jnp.float32)[:, :, None, :, None], (chans, first, BLK, second, BLK)
    )
    return wide.reshape(chans, first * BLK, second * BLK)


def outer_product(row_dir, col_dir):
    row_real = row_dir[:, 0][:, :, None, :, :, None]
    row_imag = row_dir[:, 1][:, :, None, :, :, None]
    col_real = col_dir[:, 0][:, None, :, :, None, :]
    col_imag = col_dir[:, 1][:, None, :, :, None, :]
    real_part = jnp.sum(row_real * col_real + row_imag * col_imag, axis=3)
    imag_part = jnp.sum(row_imag * col_real - row_real * col_imag, axis=3)
    return (real_part, imag_part)


def block_terms(coherency, vis_data, weight, row_gains, col_gains):
    count_dirs = row_gains.shape[4]
    chans, row_total, col_total = weight.shape
    empty = jnp.zeros((chans, 2, 2, row_total, col_total), jnp.float32)

    def model_turn(state_pair, dir_index):
        coh_dir = lax.dynamic_index_in_dim(coherency, dir_index, 1, False).astype(jnp.float32)
        coh_real = coh_dir[:, 0][:, None, None]
        coh_imag = coh_dir[:, 1][:, None, None]
        row_dir = lax.dynamic_index_in_dim(row_gains, dir_index, 4, False)
        col_dir = lax.dynamic_index_in_dim(col_gains, dir_index, 4, False)
        outer_real, outer_imag = outer_product(row_dir, col_dir)
        model_real = state_pair[0] + coh_real * outer_real - coh_imag * outer_imag
        model_imag = state_pair[1] + coh_real * outer_imag + coh_imag * outer_real
        return ((model_real, model_imag), None)

    dir_list = jnp.arange(count_dirs, dtype=jnp.int32)
    (model_real, model_imag), _ = lax.scan(model_turn, (empty, empty), dir_list)
    observed = vis_data.astype(jnp.float32)
    res_real = weight[:, None, None] * (observed[:, 0] - model_real)
    res_imag = weight[:, None, None] * (observed[:, 1] - model_imag)
    total_sq = jnp.sum(res_real * res_real + res_imag * res_imag)
    wide_real = res_real[:, :, :, None]
    wide_imag = res_imag[:, :, :, None]

    def gradient_turn(state_dummy, dir_index):
        coh_dir = lax.dynamic_index_in_dim(coherency, dir_index, 1, False).astype(jnp.float32)
        coh_real = coh_dir[:, 0][:, None, None]
        coh_imag = coh_dir[:, 1][:, None, None]
        row_dir = lax.dynamic_index_in_dim(row_gains, dir_index, 4, False)
        col_dir = lax.dynamic_index_in_dim(col_gains, dir_index, 4, False)
        col_real = col_dir[:, 0][:, None, :, :, None, :]
        col_imag = col_dir[:, 1][:, None, :, :, None, :]
        prod_real = jnp.sum(wide_real * col_real - wide_imag * col_imag, axis=2)
        prod_imag = jnp.sum(wide_real * col_imag + wide_imag * col_real, axis=2)
        row_grad_real = -jnp.sum(coh_real * prod_real + coh_imag * prod_imag, axis=-1)
        row_grad_imag = -jnp.sum(coh_real * prod_imag - coh_imag * prod_real, axis=-1)
        row_real = row_dir[:, 0][:, :, None, :, :, None]
        row_imag = row_dir[:, 1][:, :, None, :, :, None]
        herm_real = jnp.sum(wide_real * row_real + wide_imag * row_imag, axis=1)
        herm_imag = jnp.sum(wide_real * row_imag - wide_imag * row_real, axis=1)
        col_grad_real = -jnp.sum(coh_real * herm_real - coh_imag * herm_imag, axis=-2)
        col_grad_imag = -jnp.sum(coh_real * herm_imag + coh_imag * herm_real, axis=-2)
        power = weight * (coh_dir[:, 0] * coh_dir[:, 0] + coh_dir[:, 1] * coh_dir[:, 1])
        col_norm = jnp.sum(col_dir * col_dir, axis=(1, 2, 3))
        row_norm = jnp.sum(row_dir * row_dir, axis=(1, 2, 3))
        row_curv = jnp.sum(power * col_norm[:, None, :], axis=-1)
        col_curv = jnp.sum(power * row_norm[:, :, None], axis=-2)
        row_grad = jnp.stack([row_grad_real, row_grad_imag], axis=1)
        col_grad = jnp.stack([col_grad_real, col_grad_imag], axis=1)
        return (state_dummy, (row_grad, row_curv, col_grad, col_curv))

    _, stacked = lax.scan(gradient_turn, jnp.float32(0.0), dir_list)
    row_grad = jnp.moveaxis(stacked[0], 0, 4)
    row_curv = jnp.moveaxis(stacked[1], 0, 1)
    col_grad = jnp.moveaxis(stacked[2], 0, 4)
    col_curv = jnp.moveaxis(stacked[3], 0, 1)
    return (total_sq, row_grad, row_curv, col_grad, col_curv)


def on_device(gains, coherency, vis_data, flags, beam, group_of):
    chan_dev = gains.shape[0]
    row_count = gains.shape[5]
    stn_count = lax.axis_size("stn")
    stn_index = lax.axis_index("stn")
    all_stations = row_count * stn_count
    all_channels = chan_dev * lax.axis_size("chan")
    factor = beam_factor(beam, group_of)
    row_factor = lax.dynamic_slice_in_dim(factor, stn_index * row_count, row_count, 1)
    row_gains = gains * row_factor
    row_ids = stn_index * row_count + jnp.arange(row_count, dtype=jnp.int32)
    col_ids = jnp.arange(all_stations, dtype=jnp.int32)
    weight = expand_flags(flags) * (row_ids[:, None] != col_ids[None, :]).astype(jnp.float32)[None]
    local_count = jnp.sum(weight)
    all_gains = lax.all_gather(row_gains, "stn", axis=5, tiled=True)
    total_sq, row_grad, row_curv, col_grad, col_curv = block_terms(
        coherency, vis_data, weight, row_gains, all_gains
    )
    own_grad, own_curv = (
        lax.psum_scatter(col_grad, "stn", scatter_dimension=5, tiled=True),
        lax.psum_scatter(col_curv, "stn", scatter_dimension=2, tiled=True),
    )
    extended = padded(gains, (("chan", 0),), 2)
    second = extended[2:] - 2.0 * extended[1:-1] + extended[:-2]
    first_chan = lax.axis_index("chan") * chan_dev
    positions = first_chan - 1 + jnp.arange(chan_dev + 2, dtype=jnp.int32)
    inside = ((positions >= 1) & (positions <= all_channels - 2)).astype(jnp.float32)
    second = second * inside[:, None, None, None, None, None]
    smooth_grad = second[:-2] - 2.0 * second[1:-1] + second[2:]
    own_second = second[1:-1]
    smooth_local = jnp.sum(own_second * own_second)
    count_total, sq_total, smooth_total = lax.psum(
        (local_count, total_sq, smooth_local), ("chan", "stn")
    )
    norm_scale = all_channels * all_stations / count_total
    gradient = norm_scale * row_factor * (row_grad + own_grad) + smooth_weight * smooth_grad
    curvature = norm_scale * row_factor * row_factor * (row_curv + own_curv) + damping
    gain_step = gradient / curvature[:, None, None, None]
    loss_value = (norm_scale * sq_total + smooth_weight * smooth_total) / (
        all_channels * all_stations
    )
    return (gain_step, loss_value)


def solution(mesh):
    in_specs = (
        P("chan", None, None, None, None, "stn"),
        P("chan", None, None, "stn", None),
        P("chan", None, None, None, "stn", None),
        P("chan", "stn", None),
        P(),
        P(),
    )
    out_specs = (P("chan", None, None, None, None, "stn"), P())
    return jax.shard_map(
        on_device, mesh=mesh, in_specs=in_specs, out_specs=out_specs, check_vma=False
    )
```

profile of v0, /device:TPU:0, one launch (start us, length us, event | category | flops | bytes accessed | tf_op | source)
XLA Modules:
  0.0 723.5 jit_solution(1639739617188992389)
XLA Ops:
  10.3 9.2 %all_gather.3 = f32[2,2,2,2,16,512]{5,3,2,0,1,4:T(2,128)} all-gather(f32[2,2,2,2,16,128]{5,3,2,0,1,4:T(2,128)S(1)} %copy_multiply_fusion), channel_id=1, replica_groups=mesh['chan'=8,'stn'=4] {'stn'}, dimensions={5}, use_global_device_ids=true | all-gather | bytes 655360 | tf_op jit(solution)/shard_map/all_gather | solution.py:128
  19.6 7.6 %copy.35 = bf16[2,16,2,128,512]{4,3,0,2,1:T(8,128)(2,1)} copy(bf16[2,16,2,128,512]{4,3,2,1,0:T(8,128)(2,1)} %param.11) | data formatting | bytes 16777216
  27.2 213.4 %while.31 = (s32[]{:T(128)}, f32[2,2,2,128,512]{4,3,2,1,0:T(8,128)}, f32[2,2,2,128,512]{4,3,2,1,0:T(8,128)}, s32[16]{0:T(128)S(1)}, bf16[2,16,2,128,512]{4,3,0,2...) while((s32[]{:T(128)}, ...), condition=%wide.region_6.7_spmd.clone, body=%wide.region_3.6_spmd.clone.sunk | while | flops 12845062 | bytes 21700776 | solution.py:71
  34.5 4.8 fusion.24
  46.7 6.1 fusion.24
  60.1 6.1 fusion.24
  73.5 6.1 fusion.24
  86.9 6.1 fusion.24
  100.3 6.1 fusion.24
  113.7 6.1 fusion.24
  127.1 6.1 fusion.24
  140.6 6.1 fusion.24
  154.0 6.1 fusion.24
  167.4 6.1 fusion.24
  180.8 6.1 fusion.24
  194.2 6.1 fusion.24
  207.6 6.1 fusion.24
  221.0 6.1 fusion.24
  234.5 6.1 fusion.24
  243.2 4.7 reshape.125
  253.7 394.5 %while.30 = (s32[]{:T(128)}, f32[16,2,2,2,2,128]{5,0,4,3,2,1:T(8,128)}, f32[16,2,128]{2,1,0:T(2,128)}, f32[16,2,2,2,2,512]{5,0,4,3,2,1:T(8,128)}, f32[16,2,512]{...) while((s32[]{:T(128)}, ...), condition=%wide.region_20.21_spmd.clone, body=%wide.region_7.20_spmd.clone.sunk | while | flops 24538628 | bytes 30748944 | solution.py:106
  257.7 4.5 subtract_reduce_fusion.7
  270.8 5.1 reshape.137
  282.4 4.5 subtract_reduce_fusion.7
  295.4 5.1 reshape.137
  307.0 4.5 subtract_reduce_fusion.7
  320.1 5.1 reshape.137
  344.7 5.1 reshape.137
  356.3 4.5 subtract_reduce_fusion.7
  369.4 5.1 reshape.137
  394.0 5.1 reshape.137
  418.6 5.1 reshape.137
  430.3 4.5 subtract_reduce_fusion.7
  443.3 5.1 reshape.137
  454.9 4.5 subtract_reduce_fusion.7
  468.0 5.1 reshape.137
  492.7 5.1 reshape.137
  517.4 5.1 reshape.137
  529.0 4.5 subtract_reduce_fusion.7
  542.0 5.1 reshape.137
  566.6 5.1 reshape.137
  578.3 4.5 subtract_reduce_fusion.7
  591.3 5.1 reshape.137
  616.0 5.1 reshape.137
  627.6 4.5 subtract_reduce_fusion.7
  640.7 5.1 reshape.137
  658.1 4.6 collective-permute-start.1
  668.0 41.3 %all-reduce = (f32[]{:T(128)}, f32[]{:T(128)}, f32[]{:T(128)}) all-reduce(f32[]{:T(128)} %multiply_reduce_fusion.4, f32[]{:T(128)} %get-tuple-element.326, f32[]{:T(128)} %multiply_reduce_fusion.6), channel_id=1, replica_groups=mesh['chan'=8,'stn'=4] {'chan','stn'}, use_global_device_ids=true, to_apply=%region_1.0 | all-reduce | flops 3 | bytes 24 | tf_op jit(solution)/shard_map/psum | solution.py:145
  (578 shorter events, 361.7 us)
Async XLA Ops:
  7.2 702.1 %reduce-scatter.7.cloned.1.call-start = ((), (), s32[]{:S(2)}) async-start(), calls=%async_computation.3 | async-start | bytes 327680
  8.8 0.6 copy-start.7
  27.2 213.5 %copy-start.9 = (s32[2,8,32]{2,1,0:T(8,128)S(1)}, s32[2,8,32]{2,1,0:T(8,128)}, u32[]{:S(2)}) copy-start(s32[2,8,32]{2,1,0:T(8,128)} %param.13) | copy-start | bytes 6148
  243.2 4.7 copy-start.2
  247.9 1.6 copy-start
  247.9 2.2 copy-start.1
  253.7 8.5 %copy-start.3 = (f32[2,2,2,2,16,128]{5,3,2,0,1,4:T(2,128)}, f32[2,2,2,2,16,128]{5,3,2,0,1,4:T(2,128)S(1)}, u32[]{:S(2)}) copy-start(f32[2,2,2,2,16,128]{5,3,2,0,1,4:T(2,128)S(1)} %get-tuple-element.593) | copy-start | bytes 393220 | tf_op jit(solution)/shard_map/while
  270.8 7.6 %copy-start.4 = (f32[2,2,2,2,16,128]{5,3,2,0,1,4:T(2,128)S(1)}, f32[2,2,2,2,16,128]{5,3,2,0,1,4:T(2,128)}, u32[]{:S(2)}) copy-start(f32[2,2,2,2,16,128]{5,3,2,0,1,4:T(2,128)} %copy-done.3) | copy-start | bytes 393220 | tf_op jit(solution)/shard_map/while
  278.4 8.5 %copy-start.3 = (f32[2,2,2,2,16,128]{5,3,2,0,1,4:T(2,128)}, f32[2,2,2,2,16,128]{5,3,2,0,1,4:T(2,128)S(1)}, u32[]{:S(2)}) copy-start(f32[2,2,2,2,16,128]{5,3,2,0,1,4:T(2,128)S(1)} %get-tuple-element.593) | copy-start | bytes 393220 | tf_op jit(solution)/shard_map/while
  295.4 7.6 %copy-start.4 = (f32[2,2,2,2,16,128]{5,3,2,0,1,4:T(2,128)S(1)}, f32[2,2,2,2,16,128]{5,3,2,0,1,4:T(2,128)}, u32[]{:S(2)}) copy-start(f32[2,2,2,2,16,128]{5,3,2,0,1,4:T(2,128)} %copy-done.3) | copy-start | bytes 393220 | tf_op jit(solution)/shard_map/while
  303.0 8.5 %copy-start.3 = (f32[2,2,2,2,16,128]{5,3,2,0,1,4:T(2,128)}, f32[2,2,2,2,16,128]{5,3,2,0,1,4:T(2,128)S(1)}, u32[]{:S(2)}) copy-start(f32[2,2,2,2,16,128]{5,3,2,0,1,4:T(2,128)S(1)} %get-tuple-element.593) | copy-start | bytes 393220 | tf_op jit(solution)/shard_map/while
  320.0 7.6 %copy-start.4 = (f32[2,2,2,2,16,128]{5,3,2,0,1,4:T(2,128)S(1)}, f32[2,2,2,2,16,128]{5,3,2,0,1,4:T(2,128)}, u32[]{:S(2)}) copy-start(f32[2,2,2,2,16,128]{5,3,2,0,1,4:T(2,128)} %copy-done.3) | copy-start | bytes 393220 | tf_op jit(solution)/shard_map/while
  327.7 8.5 %copy-start.3 = (f32[2,2,2,2,16,128]{5,3,2,0,1,4:T(2,128)}, f32[2,2,2,2,16,128]{5,3,2,0,1,4:T(2,128)S(1)}, u32[]{:S(2)}) copy-start(f32[2,2,2,2,16,128]{5,3,2,0,1,4:T(2,128)S(1)} %get-tuple-element.593) | copy-start | bytes 393220 | tf_op jit(solution)/shard_map/while
  344.7 7.6 %copy-start.4 = (f32[2,2,2,2,16,128]{5,3,2,0,1,4:T(2,128)S(1)}, f32[2,2,2,2,16,128]{5,3,2,0,1,4:T(2,128)}, u32[]{:S(2)}) copy-start(f32[2,2,2,2,16,128]{5,3,2,0,1,4:T(2,128)} %copy-done.3) | copy-start | bytes 393220 | tf_op jit(solution)/shard_map/while
  352.3 8.5 %copy-start.3 = (f32[2,2,2,2,16,128]{5,3,2,0,1,4:T(2,128)}, f32[2,2,2,2,16,128]{5,3,2,0,1,4:T(2,128)S(1)}, u32[]{:S(2)}) copy-start(f32[2,2,2,2,16,128]{5,3,2,0,1,4:T(2,128)S(1)} %get-tuple-element.593) | copy-start | bytes 393220 | tf_op jit(solution)/shard_map/while
  369.4 7.6 %copy-start.4 = (f32[2,2,2,2,16,128]{5,3,2,0,1,4:T(2,128)S(1)}, f32[2,2,2,2,16,128]{5,3,2,0,1,4:T(2,128)}, u32[]{:S(2)}) copy-start(f32[2,2,2,2,16,128]{5,3,2,0,1,4:T(2,128)} %copy-done.3) | copy-start | bytes 393220 | tf_op jit(solution)/shard_map/while
  376.9 8.5 %copy-start.3 = (f32[2,2,2,2,16,128]{5,3,2,0,1,4:T(2,128)}, f32[2,2,2,2,16,128]{5,3,2,0,1,4:T(2,128)S(1)}, u32[]{:S(2)}) copy-start(f32[2,2,2,2,16,128]{5,3,2,0,1,4:T(2,128)S(1)} %get-tuple-element.593) | copy-start | bytes 393220 | tf_op jit(solution)/shard_map/while
  394.0 7.6 %copy-start.4 = (f32[2,2,2,2,16,128]{5,3,2,0,1,4:T(2,128)S(1)}, f32[2,2,2,2,16,128]{5,3,2,0,1,4:T(2,128)}, u32[]{:S(2)}) copy-start(f32[2,2,2,2,16,128]{5,3,2,0,1,4:T(2,128)} %copy-done.3) | copy-start | bytes 393220 | tf_op jit(solution)/shard_map/while
  401.6 8.5 %copy-start.3 = (f32[2,2,2,2,16,128]{5,3,2,0,1,4:T(2,128)}, f32[2,2,2,2,16,128]{5,3,2,0,1,4:T(2,128)S(1)}, u32[]{:S(2)}) copy-start(f32[2,2,2,2,16,128]{5,3,2,0,1,4:T(2,128)S(1)} %get-tuple-element.593) | copy-start | bytes 393220 | tf_op jit(solution)/shard_map/while
  418.6 7.6 %copy-start.4 = (f32[2,2,2,2,16,128]{5,3,2,0,1,4:T(2,128)S(1)}, f32[2,2,2,2,16,128]{5,3,2,0,1,4:T(2,128)}, u32[]{:S(2)}) copy-start(f32[2,2,2,2,16,128]{5,3,2,0,1,4:T(2,128)} %copy-done.3) | copy-start | bytes 393220 | tf_op jit(solution)/shard_map/while
  426.2 8.5 %copy-start.3 = (f32[2,2,2,2,16,128]{5,3,2,0,1,4:T(2,128)}, f32[2,2,2,2,16,128]{5,3,2,0,1,4:T(2,128)S(1)}, u32[]{:S(2)}) copy-start(f32[2,2,2,2,16,128]{5,3,2,0,1,4:T(2,128)S(1)} %get-tuple-element.593) | copy-start | bytes 393220 | tf_op jit(solution)/shard_map/while
  443.3 7.6 %copy-start.4 = (f32[2,2,2,2,16,128]{5,3,2,0,1,4:T(2,128)S(1)}, f32[2,2,2,2,16,128]{5,3,2,0,1,4:T(2,128)}, u32[]{:S(2)}) copy-start(f32[2,2,2,2,16,128]{5,3,2,0,1,4:T(2,128)} %copy-done.3) | copy-start | bytes 393220 | tf_op jit(solution)/shard_map/while
  450.9 8.5 %copy-start.3 = (f32[2,2,2,2,16,128]{5,3,2,0,1,4:T(2,128)}, f32[2,2,2,2,16,128]{5,3,2,0,1,4:T(2,128)S(1)}, u32[]{:S(2)}) copy-start(f32[2,2,2,2,16,128]{5,3,2,0,1,4:T(2,128)S(1)} %get-tuple-element.593) | copy-start | bytes 393220 | tf_op jit(solution)/shard_map/while
  468.0 7.6 %copy-start.4 = (f32[2,2,2,2,16,128]{5,3,2,0,1,4:T(2,128)S(1)}, f32[2,2,2,2,16,128]{5,3,2,0,1,4:T(2,128)}, u32[]{:S(2)}) copy-start(f32[2,2,2,2,16,128]{5,3,2,0,1,4:T(2,128)} %copy-done.3) | copy-start | bytes 393220 | tf_op jit(solution)/shard_map/while
  475.6 8.5 %copy-start.3 = (f32[2,2,2,2,16,128]{5,3,2,0,1,4:T(2,128)}, f32[2,2,2,2,16,128]{5,3,2,0,1,4:T(2,128)S(1)}, u32[]{:S(2)}) copy-start(f32[2,2,2,2,16,128]{5,3,2,0,1,4:T(2,128)S(1)} %get-tuple-element.593) | copy-start | bytes 393220 | tf_op jit(solution)/shard_map/while
  492.7 7.6 %copy-start.4 = (f32[2,2,2,2,16,128]{5,3,2,0,1,4:T(2,128)S(1)}, f32[2,2,2,2,16,128]{5,3,2,0,1,4:T(2,128)}, u32[]{:S(2)}) copy-start(f32[2,2,2,2,16,128]{5,3,2,0,1,4:T(2,128)} %copy-done.3) | copy-start | bytes 393220 | tf_op jit(solution)/shard_map/while
  500.3 8.5 %copy-start.3 = (f32[2,2,2,2,16,128]{5,3,2,0,1,4:T(2,128)}, f32[2,2,2,2,16,128]{5,3,2,0,1,4:T(2,128)S(1)}, u32[]{:S(2)}) copy-start(f32[2,2,2,2,16,128]{5,3,2,0,1,4:T(2,128)S(1)} %get-tuple-element.593) | copy-start | bytes 393220 | tf_op jit(solution)/shard_map/while
  517.4 7.6 %copy-start.4 = (f32[2,2,2,2,16,128]{5,3,2,0,1,4:T(2,128)S(1)}, f32[2,2,2,2,16,128]{5,3,2,0,1,4:T(2,128)}, u32[]{:S(2)}) copy-start(f32[2,2,2,2,16,128]{5,3,2,0,1,4:T(2,128)} %copy-done.3) | copy-start | bytes 393220 | tf_op jit(solution)/shard_map/while
  524.9 8.5 %copy-start.3 = (f32[2,2,2,2,16,128]{5,3,2,0,1,4:T(2,128)}, f32[2,2,2,2,16,128]{5,3,2,0,1,4:T(2,128)S(1)}, u32[]{:S(2)}) copy-start(f32[2,2,2,2,16,128]{5,3,2,0,1,4:T(2,128)S(1)} %get-tuple-element.593) | copy-start | bytes 393220 | tf_op jit(solution)/shard_map/while
  542.0 7.5 %copy-start.4 = (f32[2,2,2,2,16,128]{5,3,2,0,1,4:T(2,128)S(1)}, f32[2,2,2,2,16,128]{5,3,2,0,1,4:T(2,128)}, u32[]{:S(2)}) copy-start(f32[2,2,2,2,16,128]{5,3,2,0,1,4:T(2,128)} %copy-done.3) | copy-start | bytes 393220 | tf_op jit(solution)/shard_map/while
  549.6 8.5 %copy-start.3 = (f32[2,2,2,2,16,128]{5,3,2,0,1,4:T(2,128)}, f32[2,2,2,2,16,128]{5,3,2,0,1,4:T(2,128)S(1)}, u32[]{:S(2)}) copy-start(f32[2,2,2,2,16,128]{5,3,2,0,1,4:T(2,128)S(1)} %get-tuple-element.593) | copy-start | bytes 393220 | tf_op jit(solution)/shard_map/while
  566.6 7.6 %copy-start.4 = (f32[2,2,2,2,16,128]{5,3,2,0,1,4:T(2,128)S(1)}, f32[2,2,2,2,16,128]{5,3,2,0,1,4:T(2,128)}, u32[]{:S(2)}) copy-start(f32[2,2,2,2,16,128]{5,3,2,0,1,4:T(2,128)} %copy-done.3) | copy-start | bytes 393220 | tf_op jit(solution)/shard_map/while
  574.3 8.5 %copy-start.3 = (f32[2,2,2,2,16,128]{5,3,2,0,1,4:T(2,128)}, f32[2,2,2,2,16,128]{5,3,2,0,1,4:T(2,128)S(1)}, u32[]{:S(2)}) copy-start(f32[2,2,2,2,16,128]{5,3,2,0,1,4:T(2,128)S(1)} %get-tuple-element.593) | copy-start | bytes 393220 | tf_op jit(solution)/shard_map/while
  591.3 7.6 %copy-start.4 = (f32[2,2,2,2,16,128]{5,3,2,0,1,4:T(2,128)S(1)}, f32[2,2,2,2,16,128]{5,3,2,0,1,4:T(2,128)}, u32[]{:S(2)}) copy-start(f32[2,2,2,2,16,128]{5,3,2,0,1,4:T(2,128)} %copy-done.3) | copy-start | bytes 393220 | tf_op jit(solution)/shard_map/while
  598.9 8.5 %copy-start.3 = (f32[2,2,2,2,16,128]{5,3,2,0,1,4:T(2,128)}, f32[2,2,2,2,16,128]{5,3,2,0,1,4:T(2,128)S(1)}, u32[]{:S(2)}) copy-start(f32[2,2,2,2,16,128]{5,3,2,0,1,4:T(2,128)S(1)} %get-tuple-element.593) | copy-start | bytes 393220 | tf_op jit(solution)/shard_map/while
  616.0 7.6 %copy-start.4 = (f32[2,2,2,2,16,128]{5,3,2,0,1,4:T(2,128)S(1)}, f32[2,2,2,2,16,128]{5,3,2,0,1,4:T(2,128)}, u32[]{:S(2)}) copy-start(f32[2,2,2,2,16,128]{5,3,2,0,1,4:T(2,128)} %copy-done.3) | copy-start | bytes 393220 | tf_op jit(solution)/shard_map/while
  623.6 8.5 %copy-start.3 = (f32[2,2,2,2,16,128]{5,3,2,0,1,4:T(2,128)}, f32[2,2,2,2,16,128]{5,3,2,0,1,4:T(2,128)S(1)}, u32[]{:S(2)}) copy-start(f32[2,2,2,2,16,128]{5,3,2,0,1,4:T(2,128)S(1)} %get-tuple-element.593) | copy-start | bytes 393220 | tf_op jit(solution)/shard_map/while
  640.7 7.6 %copy-start.4 = (f32[2,2,2,2,16,128]{5,3,2,0,1,4:T(2,128)S(1)}, f32[2,2,2,2,16,128]{5,3,2,0,1,4:T(2,128)}, u32[]{:S(2)}) copy-start(f32[2,2,2,2,16,128]{5,3,2,0,1,4:T(2,128)} %copy-done.3) | copy-start | bytes 393220 | tf_op jit(solution)/shard_map/while
  652.4 4.4 copy-start.5
  656.7 57.2 %reduce-scatter.5.cloned.1.call-start = ((), (), s32[]{:S(2)}) async-start(), calls=%async_computation.2 | async-start | bytes 655360 | tf_op jit(solution)/shard_map/reduce_scatter | solution.py:133
  656.8 8.0 %collective-permute-start = (f32[2,2,2,2,16,128]{5,4,3,2,1,0:T(8,128)S(1)}, f32[2,2,2,2,16,128]{5,4,3,2,1,0:T(8,128)S(1)}, u32[]{:S(2)}, u32[]{:S(2)}) collective-permute-start(f32[2,2,2,2,16,128]{5,4,3,2,1,0:T(8,128)S(1)} %copy-done.5), channel_id=1, source_target_pairs={{4,0},{8,4},{12,8},{16,12},{20,16},{24,20},{28,24},{5,1},{9,5},{13... | collective-permute-start | bytes 393224 | tf_op jit(solution)/shard_map/ppermute | solution.py:23
  658.1 9.1 %collective-permute-start.1 = (f32[2,2,2,2,16,128]{5,4,3,2,1,0:T(8,128)S(1)}, f32[2,2,2,2,16,128]{5,4,3,2,1,0:T(8,128)S(1)}, u32[]{:S(2)}, u32[]{:S(2)}) collective-permute-start(f32[2,2,2,2,16,128]{5,4,3,2,1,0:T(8,128)S(1)} %copy-done.5), channel_id=1, source_target_pairs={{0,4},{4,8},{8,12},{12,16},{16,20},{20,24},{24,28},{1,5},{5,9},{9,... | collective-permute-start | bytes 393224 | tf_op jit(solution)/shard_map/ppermute | solution.py:21
  662.9 50.2 %copy-start.8 = (f32[16,2,128]{2,1,0:T(2,128)S(1)}, f32[16,2,128]{2,1,0:T(2,128)}, u32[]{:S(2)}) copy-start(f32[16,2,128]{2,1,0:T(2,128)} %get-tuple-element.109) | copy-start | bytes 49156
  662.9 51.0 %copy-start.6 = (f32[16,2,2,2,2,128]{5,0,4,3,2,1:T(8,128)S(1)}, f32[16,2,2,2,2,128]{5,0,4,3,2,1:T(8,128)}, u32[]{:S(2)}) copy-start(f32[16,2,2,2,2,128]{5,0,4,3,2,1:T(8,128)} %get-tuple-element.107) | copy-start | bytes 393220
Sparse Core Ops, SparseCore 0:
  656.8 21.0 reduce-scatter.6
  680.6 21.6 reduce-scatter.4
where the time goes:
time: 731 us; the launch traced here: 723 us
  other arithmetic  321 us (44%)
  local copies, waits for them, and re-layouts  267 us (37%)
  loops' own time  58.6 us (8%)
  blocking collectives  50.6 us (7%)
  between operations  17.4 us (2%)
    add x16, other arithmetic, model_turn(): model_imag = state_pair[1] + coh_real * outer_imag + coh_imag * outer_real  96 us
    reshape x17, local copies, waits for them, and re-layouts, expand_flags(): return wide.reshape(chans, first * BLK, second * BLK)  87 us
    dynamic_update_slice x96, local copies, waits for them, and re-layouts, block_terms(): _, stacked = lax.scan(gradient_turn, jnp.float32(0.0), dir_list)  71.8 us
    reduce_sum x16, other arithmetic, gradient_turn(): herm_imag = jnp.sum(wide_real * row_imag - wide_imag * row_real, axis=1)  71.3 us
    reduce_sum x16, other arithmetic, outer_product(): real_part = jnp.sum(row_real * col_real + row_imag * col_imag, axis=3)  49.6 us
    broadcast_in_dim x17, local copies, waits for them, and re-layouts, expand_flags(): jnp.broadcast_to(flags.astype(jnp.float32)[:, :, None, :, None], (chans,...  43.7 us
    psum x1, blocking collectives, on_device(): lax.psum((local_count, total_sq, smooth_local), ('chan', 'stn'))  41.3 us
    another operation x1, loops' own time, block_terms(): _, stacked = lax.scan(gradient_turn, jnp.float32(0.0), dir_list)  31.8 us
  transfers between devices with their start and end apart: 4, of which 1 were waited for; matrix products, arithmetic and copies ran while one was open for 1% of the time, Pallas kernels for 0%

commit v1 on v0

v1 whole, which is shorter than its diff:
```python
import functools

import jax
import jax.numpy as jnp
from jax import lax
from jax.experimental import pallas as pl
from jax.experimental.pallas import tpu as pltpu
from jax.sharding import PartitionSpec as P

smooth_weight = 0.05
damping = 0.3
GROUP = 2
ROWS = 16


def split_pair(values):
    high = values.astype(jnp.bfloat16).astype(jnp.float32)
    return high, values - high


def dot_nn(left, right):
    return lax.dot_general(left, right, (((1,), (0,)), ((), ())), preferred_element_type=jnp.float32)


def dot_nt(left, right):
    return lax.dot_general(left, right, (((1,), (1,)), ((), ())), preferred_element_type=jnp.float32)


def dot_tn(left, right):
    return lax.dot_general(left, right, (((0,), (0,)), ((), ())), preferred_element_type=jnp.float32)


def turned(four):
    return jnp.concatenate([-four[2:4], four[0:2]], axis=0)


def kernel(
    coh, vis, flags, row_j, col_j,
    row_out, col_out, stat_out,
    right_s, left_s, norm_q, norm_p, weight_s, res, outer0, outer1,
    ehi0, elo0, ehi1, elo1, phi0, plo0, phi1, plo1,
):
    dirs = coh.shape[1]
    rows, cols = coh.shape[3], coh.shape[4]
    blocks_r, blocks_c = flags.shape[1], flags.shape[2]
    blk = cols // blocks_c

    def prepare(k, carry):
        xq = col_j[0, k]
        hq, lq = split_pair(xq)
        for b in range(2):
            for e in range(2):
                h, l = hq[4 * b:4 * b + 4], lq[4 * b:4 * b + 4]
                if e:
                    h, l = turned(h), turned(l)
                right_s[k, :, (2 * b + e) * cols:(2 * b + e + 1) * cols] = jnp.concatenate(
                    [h, l, h, l], axis=0).astype(jnp.bfloat16)
        xp = row_j[0, k]
        hp, lp = split_pair(xp)
        for e in range(2):
            for a in range(2):
                h, l = hp[4 * a:4 * a + 4], lp[4 * a:4 * a + 4]
                if e:
                    h, l = -turned(h), -turned(l)
                left_s[k, :, (2 * e + a) * rows:(2 * e + a + 1) * rows] = jnp.concatenate(
                    [h, h, l, l], axis=0).astype(jnp.bfloat16)
        for ref, x in ((norm_q, xq), (norm_p, xp)):
            total = jnp.sum(x * x, axis=0, keepdims=True)
            high, low = split_pair(total)
            place = lax.broadcasted_iota(jnp.int32, (16, x.shape[1]), 0)
            ref[k] = jnp.where(place == 0, high, jnp.where(place == 1, low, 0.0)).astype(jnp.bfloat16)
        return carry

    lax.fori_loop(0, dirs, prepare, 0)

    spread_c = (
        lax.broadcasted_iota(jnp.int32, (blocks_c, cols), 0)
        == lax.broadcasted_iota(jnp.int32, (blocks_c, cols), 1) // blk
    ).astype(jnp.float32)
    wide = dot_nn(flags[0].astype(jnp.float32), spread_c)
    first = lax.axis_index("stn") * rows
    count = jnp.zeros((blk, cols), jnp.float32)
    for i in range(blocks_r):
        ids = first + i * blk + lax.broadcasted_iota(jnp.int32, (blk, cols), 0)
        other = lax.broadcasted_iota(jnp.int32, (blk, cols), 1)
        w = jnp.where(ids != other, jnp.broadcast_to(wide[i:i + 1], (blk, cols)), 0.0)
        weight_s[i * blk:(i + 1) * blk, :] = w
        count = count + w
    stat_out[0, 0] = jnp.sum(count.reshape(blk // 8, 8, cols), axis=0)

    res[...] = jnp.zeros_like(res)

    def outer_of(start, outer):
        for g in range(GROUP):
            k = jnp.minimum(start + g, dirs - 1)
            left = left_s[k]
            for b in range(2):
                outer[g, :, b * cols:(b + 1) * cols] = dot_tn(
                    left, right_s[k, :, 2 * b * cols:(2 * b + 1) * cols])

    def add_model(start, outer):
        for r in range(0, rows, ROWS):
            c = [
                (coh[0, start + g, 0, r:r + ROWS, :].astype(jnp.float32),
                 coh[0, start + g, 1, r:r + ROWS, :].astype(jnp.float32))
                for g in range(GROUP)
            ]
            for a in range(2):
                for b in range(2):
                    at_r = slice(a * rows + r, a * rows + r + ROWS)
                    at_i = slice((2 + a) * rows + r, (2 + a) * rows + r + ROWS)
                    lane = slice(b * cols, (b + 1) * cols)
                    mr, mi = res[at_r, lane], res[at_i, lane]
                    for g in range(GROUP):
                        o_r, o_i = outer[g, at_r, lane], outer[g, at_i, lane]
                        cr, ci = c[g]
                        mr = mr + (cr * o_r - ci * o_i)
                        mi = mi + (cr * o_i + ci * o_r)
                    res[at_r, lane] = mr
                    res[at_i, lane] = mi

    outer_of(0, outer0)

    def model_turn(j, carry):
        at = j * (2 * GROUP)
        outer_of(at + GROUP, outer1)
        add_model(at, outer0)
        outer_of(at + 2 * GROUP, outer0)
        add_model(at + GROUP, outer1)
        return carry

    lax.fori_loop(0, dirs // (2 * GROUP), model_turn, 0)

    squares = jnp.zeros((8, cols), jnp.float32)
    for r in range(0, rows, ROWS):
        w = weight_s[r:r + ROWS, :]
        for e in range(2):
            for a in range(2):
                for b in range(2):
                    at = slice((2 * e + a) * rows + r, (2 * e + a) * rows + r + ROWS)
                    lane = slice(b * cols, (b + 1) * cols)
                    value = w * (vis[0, e, a, b, r:r + ROWS, :].astype(jnp.float32) - res[at, lane])
                    res[at, lane] = value
                    squares = squares + jnp.sum((value * value).reshape(ROWS // 8, 8, cols), axis=0)
    stat_out[0, 1] = squares

    def build(k, ehi, elo, phi, plo):
        for r in range(0, rows, ROWS):
            cr = coh[0, k, 0, r:r + ROWS, :].astype(jnp.float32)
            ci = coh[0, k, 1, r:r + ROWS, :].astype(jnp.float32)
            power = weight_s[r:r + ROWS, :] * (cr * cr + ci * ci)
            high = power.astype(jnp.bfloat16)
            phi[r:r + ROWS, :] = high
            plo[r:r + ROWS, :] = (power - high.astype(jnp.float32)).astype(jnp.bfloat16)
            for a in range(2):
                for b in range(2):
                    lane = slice(b * cols, (b + 1) * cols)
                    rr = res[a * rows + r:a * rows + r + ROWS, lane]
                    ri = res[(2 + a) * rows + r:(2 + a) * rows + r + ROWS, lane]
                    for e, value in ((0, cr * rr + ci * ri), (1, cr * ri - ci * rr)):
                        high = value.astype(jnp.bfloat16)
                        at = slice(a * rows + r, a * rows + r + ROWS)
                        to = slice((2 * b + e) * cols, (2 * b + e + 1) * cols)
                        ehi[at, to] = high
                        elo[at, to] = (value - high.astype(jnp.float32)).astype(jnp.bfloat16)

    def reduce(k, ehi, elo, phi, plo):
        right = right_s[k]
        left = left_s[k]
        row_g = dot_nt(right, ehi[...]) + dot_nt(right, elo[...])
        row_g = row_g[0:4] + row_g[4:8]
        at = pl.multiple_of(k * 8, 8)
        row_out[0, pl.ds(at, 8), :] = jnp.concatenate([row_g[:, :rows], row_g[:, rows:]], axis=0)
        parts = []
        for b in range(2):
            total = None
            for e in range(2):
                lane = slice((2 * b + e) * cols, (2 * b + e + 1) * cols)
                side = left[:, e * 2 * rows:(e + 1) * 2 * rows]
                term = dot_nn(side, ehi[:, lane]) + dot_nn(side, elo[:, lane])
                total = term if total is None else total + term
            parts.append(total[0:4] + total[8:12])
        col_out[0, pl.ds(at, 8), :] = jnp.concatenate(parts, axis=0)
        row_c = dot_nt(norm_q[k], phi[...]) + dot_nt(norm_q[k], plo[...])
        col_c = dot_nn(norm_p[k], phi[...]) + dot_nn(norm_p[k], plo[...])
        row_out[0, pl.ds(dirs * 8 + k, 1), :] = row_c[0:1] + row_c[1:2]
        col_out[0, pl.ds(dirs * 8 + k, 1), :] = col_c[0:1] + col_c[1:2]

    set0 = (ehi0, elo0, phi0, plo0)
    set1 = (ehi1, elo1, phi1, plo1)
    build(0, *set0)

    def gradient_turn(j, carry):
        reduce(2 * j, *set0)
        build(2 * j + 1, *set1)
        reduce(2 * j + 1, *set1)
        build(jnp.minimum(2 * j + 2, dirs - 1), *set0)
        return carry

    lax.fori_loop(0, dirs // 2, gradient_turn, 0)


def device_terms(coherency, vis_data, flags, row_j, col_j):
    chans, dirs, _, rows, cols = coherency.shape
    bf, f4 = jnp.bfloat16, jnp.float32

    def per_chan(shape):
        rest = len(shape) - 1
        return pl.BlockSpec((1,) + tuple(shape[1:]), lambda f: (f,) + (0,) * rest)

    outs = [
        jax.ShapeDtypeStruct((chans, dirs * 9, rows), f4),
        jax.ShapeDtypeStruct((chans, dirs * 9, cols), f4),
        jax.ShapeDtypeStruct((chans, 2, 8, cols), f4),
    ]
    ins = (coherency, vis_data, flags, row_j, col_j)
    vm = pltpu.VMEM
    return pl.pallas_call(
        kernel,
        grid=(chans,),
        in_specs=[per_chan(x.shape) for x in ins],
        out_specs=[per_chan(x.shape) for x in outs],
        out_shape=outs,
        scratch_shapes=[
            vm((dirs, 16, 4 * cols), bf),
            vm((dirs, 16, 4 * rows), bf),
            vm((dirs, 16, cols), bf),
            vm((dirs, 16, rows), bf),
            vm((rows, cols), f4),
            vm((4 * rows, 2 * cols), f4),
            vm((GROUP, 4 * rows, 2 * cols), f4),
            vm((GROUP, 4 * rows, 2 * cols), f4),
            vm((2 * rows, 4 * cols), bf),
            vm((2 * rows, 4 * cols), bf),
            vm((2 * rows, 4 * cols), bf),
            vm((2 * rows, 4 * cols), bf),
            vm((rows, cols), bf),
            vm((rows, cols), bf),
            vm((rows, cols), bf),
            vm((rows, cols), bf),
        ],
        compiler_params=pltpu.CompilerParams(vmem_limit_bytes=56 * 1024 * 1024),
    )(*ins)


def on_device(gains, coherency, vis_data, flags, beam, group_of):
    chans, dirs, rows = gains.shape[0], gains.shape[4], gains.shape[5]
    stn_count = lax.axis_size("stn")
    chan_count = lax.axis_size("chan")
    stn_index = lax.axis_index("stn")
    all_stations = rows * stn_count
    all_channels = chans * chan_count
    groups = beam.shape[0]
    own_groups = lax.dynamic_slice_in_dim(group_of, stn_index * rows, rows, 0)
    onehot = (own_groups[None, :] == jnp.arange(groups, dtype=jnp.int32)[:, None]).astype(jnp.float32)
    factor = jnp.sum(beam[:, :, None] * onehot[:, None, :], axis=0)

    own_t = jnp.transpose(gains * factor, (0, 4, 2, 1, 3, 5)).reshape(chans, dirs, 8, rows)
    all_t = lax.all_gather(own_t, "stn", axis=3, tiled=True)

    ends = chan_count - 1
    last = gains[chans - 2:]
    head = gains[:2]
    before = lax.ppermute(last, "chan", [(i, i + 1) for i in range(ends)])
    after = lax.ppermute(head, "chan", [(i + 1, i) for i in range(ends)])
    extended = jnp.concatenate([before, gains, after], axis=0)
    second = extended[2:] - 2.0 * extended[1:-1] + extended[:-2]
    first_chan = lax.axis_index("chan") * chans
    positions = first_chan - 1 + jnp.arange(chans + 2, dtype=jnp.int32)
    inside = ((positions >= 1) & (positions <= all_channels - 2)).astype(jnp.float32)
    second = second * inside[:, None, None, None, None, None]
    smooth_grad = second[:-2] - 2.0 * second[1:-1] + second[2:]
    own_second = second[1:-1]
    smooth_local = jnp.sum(own_second * own_second)

    row_out, col_out, stats = device_terms(coherency, vis_data, flags, own_t, all_t)
    summed = lax.psum_scatter(col_out, "stn", scatter_dimension=2, tiled=True) + row_out
    local = jnp.stack([jnp.sum(stats[:, 0]), jnp.sum(stats[:, 1]), smooth_local])
    count_total, sq_total, smooth_total = lax.psum(local, ("chan", "stn"))

    norm_scale = all_channels * all_stations / count_total
    grad = summed[:, :dirs * 8].reshape(chans, dirs, 2, 2, 2, rows)
    grad = -jnp.transpose(grad, (0, 3, 2, 4, 1, 5))
    curv = summed[:, dirs * 8:]
    gradient = norm_scale * factor * grad + smooth_weight * smooth_grad
    curvature = norm_scale * factor * factor * curv + damping
    gain_step = gradient / curvature[:, None, None, None]
    loss_value = (norm_scale * sq_total + smooth_weight * smooth_total) / (
        all_channels * all_stations
    )
    return (gain_step, loss_value)


def solution(mesh):
    in_specs = (
        P("chan", None, None, None, None, "stn"),
        P("chan", None, None, "stn", None),
        P("chan", None, None, None, "stn", None),
        P("chan", "stn", None),
        P(),
        P(),
    )
    out_specs = (P("chan", None, None, None, None, "stn"), P())
    return jax.shard_map(
        on_device, mesh=mesh, in_specs=in_specs, out_specs=out_specs, check_vma=False
    )
```

time: 731 us -> 146 us (0.20); the launches traced: 723 us -> 146 us
  other arithmetic: 321 us -> 7.53 us
  local copies, waits for them, and re-layouts: 267 us -> 1.43 us
  Pallas kernels: 0 us -> 60.5 us
  loops' own time: 58.6 us -> 0 us
    reduce_sum x99 -> x2, other arithmetic: 182 us -> 2.17 us  [the longest x1 1.4 us: on_device(): jnp.sum(stats[:, 0])]
    add x19 -> x2, other arithmetic: 96 us -> 1.01 us  [the longest x1 1 us: on_device(): lax.psum_scatter(col_out, 'stn', scatter_dimension=2, tiled=True) + row_out]
    reshape x17 -> x0, local copies, waits for them, and re-layouts: 87 us -> none  [expand_flags(): return wide.reshape(chans, first * BLK, second * BLK)]
    dynamic_update_slice x96 -> x0, local copies, waits for them, and re-layouts: 71.8 us -> none  [block_terms(): _, stacked = lax.scan(gradient_turn, jnp.float32(0.0), dir_list)]
    pallas_call x0 -> x1, Pallas kernels: none -> 60.5 us  [device_terms(): pl.pallas_call(kernel, grid=(chans,), in_specs=[per_chan(x.shape) for x i...]
    another operation x2 -> x0, loops' own time: 58.6 us -> none  [the longest x1 31.8 us: block_terms(): _, stacked = lax.scan(gradient_turn, jnp.float32(0.0), dir_list)]
    broadcast_in_dim x17 -> x0, local copies, waits for them, and re-layouts: 43.7 us -> none  [expand_flags(): jnp.broadcast_to(flags.astype(jnp.float32)[:, :, None, :, None], (chans,...]
    convert_element_type x37 -> x1, other arithmetic: 38.8 us -> 0.01 us  [on_device(): (own_groups[None, :] == jnp.arange(groups, dtype=jnp.int32)[:, None]).ast...]
  transfers between devices with their start and end apart: 4 -> 3, of which waited for: 1 -> 2; matrix products, arithmetic and copies ran while one was open for 1% -> 3% of each run, Pallas kernels for 0% -> 0%
where the time goes in v1:
time: 146 us
  Pallas kernels  60.5 us (41%)
  blocking collectives  50.2 us (34%)
  between operations  17.2 us (12%)
  other arithmetic  7.53 us (5%)
  starting transfers between devices  5.88 us (4%)
  waiting for transfers between devices  3.11 us (2%)
    pallas_call x1, Pallas kernels, device_terms(): pl.pallas_call(kernel, grid=(chans,), in_specs=[per_chan(x.shape) for x i...  60.5 us
    psum x1, blocking collectives, on_device(): count_total, sq_total, smooth_total = lax.psum(local, ('chan', 'stn'))  41 us
    all_gather x1, blocking collectives, on_device(): all_t = lax.all_gather(own_t, 'stn', axis=3, tiled=True)  9.11 us
    ppermute x1, starting transfers between devices, on_device(): before = lax.ppermute(last, 'chan', [(i, i + 1) for i in range(ends)])  4.55 us
  transfers between devices with their start and end apart: 3, of which 2 were waited for; matrix products, arithmetic and copies ran while one was open for 3% of the time, Pallas kernels for 0%

profile of v1, /device:TPU:0, one launch (start us, length us, event | category | flops | bytes accessed | tf_op | source)
XLA Modules:
  0.0 145.9 jit_solution(18370645099635069984)
XLA Ops:
  7.2 0.0 copy-start.1
  7.2 0.0 reduce-scatter.2.cloned.1.call-start
  7.2 0.8 dynamic_slice.3
  8.0 0.8 multiply_reduce_fusion.1
  8.8 0.9 multiply_bitcast_fusion
  9.7 0.1 copy.10
  9.8 0.0 copy-start
  9.8 9.1 %all_gather.3.col_j = f32[2,16,8,512]{3,2,1,0:T(8,128)} all-gather(f32[2,16,8,128]{3,2,1,0:T(8,128)S(1)} %bitcast.12), channel_id=1, replica_groups=mesh['chan'=8,'stn'=4] {'stn'}, dimensions={3}, use_global_device_ids=true | all-gather | bytes 655360 | tf_op jit(solution)/shard_map/all_gather | solution.py:259
  18.9 0.0 copy-done
  18.9 60.5 %shard_map.77 = (f32[2,144,128]{2,1,0:T(8,128)}, f32[2,144,512]{2,1,0:T(8,128)}, f32[2,2,8,512]{3,2,1,0:T(8,128)}) custom-call(bf16[2,16,2,128,512]{4,3,2,1,0:T(8,128)(2,1)} %coh.1, bf16[2,2,2,2,128,512]{5,4,3,2,1,0:T(8,128)(2,1)} %vis.1, s32[2,8,32]{2,1,0:T(8,128)} %flags.1, f32[2,16,8,128]{3,2,1,0:T(8,128)} %bitcast.13, f32[2,16,8,512]{3,2,1,0:T(8,128)} %all_gather.3.col_j), custom_call_target="tpu_custom_call" | custom-call | tf_op jit(solution)/shard_map/pallas_call | solution.py:218
  79.4 0.0 reduce-scatter.2.cloned.1.call-update
  79.5 0.0 copy-done.1
  79.5 1.3 collective-permute-start
  80.8 4.6 %collective-permute-start.1 = (f32[2,2,2,2,16,128]{5,4,3,2,1,0:T(8,128)S(1)}, f32[2,2,2,2,16,128]{5,4,3,2,1,0:T(8,128)S(1)}, u32[]{:S(2)}, u32[]{:S(2)}) collective-permute-start(f32[2,2,2,2,16,128]{5,4,3,2,1,0:T(8,128)S(1)} %copy-done.1), channel_id=1, source_target_pairs={{0,4},{4,8},{8,12},{12,16},{16,20},{20,24},{24,28},{1,5},{5,9},{9,... | collective-permute-start | bytes 393224 | tf_op jit(solution)/shard_map/ppermute | solution.py:264
  85.3 1.4 slice_reduce_fusion.1
  86.7 0.4 collective-permute-done
  87.1 2.7 %collective-permute-done.1 = f32[2,2,2,2,16,128]{5,4,3,2,1,0:T(8,128)S(1)} collective-permute-done((f32[2,2,2,2,16,128]{5,4,3,2,1,0:T(8,128)S(1)}, f32[2,2,2,2,16,128]{5,4,3,2,1,0:T(8,128)S(1)}, u32[]{:S(2)}, u32[]{:S(2)}) %collective-permute-start.1) | collective-permute-done | bytes 131104 | tf_op jit(solution)/shard_map/ppermute | solution.py:264
  89.8 0.1 fusion.3
  89.9 0.6 multiply_reduce_fusion
  90.5 2.0 %pad_maximum_fusion.2 = f32[3]{0:T(128)S(1)} fusion(f32[1]{0:T(128)} %bitcast.4, f32[1]{0:T(128)} %bitcast.3, f32[1]{0:T(128)} %bitcast.2), kind=kLoop, calls=%fused_computation.25 | loop fusion | flops 6 | bytes 24 | tf_op jit(solution)/shard_map/stack | solution.py:278
  92.5 41.0 %psum.7 = f32[3]{0:T(128)S(1)} all-reduce(f32[3]{0:T(128)S(1)} %pad_maximum_fusion.2), channel_id=1, replica_groups=mesh['chan'=8,'stn'=4] {'chan','stn'}, use_global_device_ids=true, to_apply=%region_4.0 | all-reduce | flops 3 | bytes 24 | tf_op jit(solution)/shard_map/psum | solution.py:279
  133.6 0.6 fusion.10
  136.1 0.0 reduce-scatter.2.cloned.1.call-done
  136.2 1.0 add.43
  137.2 0.7 fusion.6
  (5 shorter events, 0.0 us)
Async XLA Ops:
  7.2 72.3 %copy-start.1 = (f32[2,2,2,2,16,128]{5,4,3,2,1,0:T(8,128)S(1)}, f32[2,2,2,2,16,128]{5,4,3,2,1,0:T(8,128)}, u32[]{:S(2)}) copy-start(f32[2,2,2,2,16,128]{5,4,3,2,1,0:T(8,128)} %param.6) | copy-start | bytes 393220
  7.2 129.0 %reduce-scatter.2.cloned.1.call-start = ((), (), s32[]{:S(2)}) async-start(), calls=%async_computation.1 | async-start | bytes 737280 | tf_op jit(solution)/shard_map/reduce_scatter | solution.py:277
  9.8 9.1 %copy-start = (f32[2,16,2,2,2,128]{5,4,3,2,1,0:T(2,128)}, f32[2,16,2,2,2,128]{5,4,3,2,1,0:T(2,128)S(1)}, u32[]{:S(2)}) copy-start(f32[2,16,2,2,2,128]{5,4,3,2,1,0:T(2,128)S(1)} %copy.10) | copy-start | bytes 393220
  79.5 7.6 %collective-permute-start = (f32[2,2,2,2,16,128]{5,4,3,2,1,0:T(8,128)S(1)}, f32[2,2,2,2,16,128]{5,4,3,2,1,0:T(8,128)S(1)}, u32[]{:S(2)}, u32[]{:S(2)}) collective-permute-start(f32[2,2,2,2,16,128]{5,4,3,2,1,0:T(8,128)S(1)} %copy-done.1), channel_id=1, source_target_pairs={{4,0},{8,4},{12,8},{16,12},{20,16},{24,20},{28,24},{5,1},{9,5},{13... | collective-permute-start | bytes 393224 | tf_op jit(solution)/shard_map/ppermute | solution.py:265
  80.8 9.1 %collective-permute-start.1 = (f32[2,2,2,2,16,128]{5,4,3,2,1,0:T(8,128)S(1)}, f32[2,2,2,2,16,128]{5,4,3,2,1,0:T(8,128)S(1)}, u32[]{:S(2)}, u32[]{:S(2)}) collective-permute-start(f32[2,2,2,2,16,128]{5,4,3,2,1,0:T(8,128)S(1)} %copy-done.1), channel_id=1, source_target_pairs={{0,4},{4,8},{8,12},{12,16},{16,20},{20,24},{24,28},{1,5},{5,9},{9,... | collective-permute-start | bytes 393224 | tf_op jit(solution)/shard_map/ppermute | solution.py:264
Sparse Core Ops, SparseCore 0:
  79.6 23.1 reduce-scatter.1

commit v2 on v1

--- a/solution.py
+++ b/solution.py
@@ -35,7 +35,7 @@
 
 
 def kernel(
-    coh, vis, flags, row_j, col_j,
+    coh, vis, flags, col_j,
     row_out, col_out, stat_out,
     right_s, left_s, norm_q, norm_p, weight_s, res, outer0, outer1,
     ehi0, elo0, ehi1, elo1, phi0, plo0, phi1, plo1,
@@ -44,6 +44,7 @@
     rows, cols = coh.shape[3], coh.shape[4]
     blocks_r, blocks_c = flags.shape[1], flags.shape[2]
     blk = cols // blocks_c
+    first = pl.multiple_of(lax.axis_index("stn") * rows, 128)
 
     def prepare(k, carry):
         xq = col_j[0, k]
@@ -55,7 +56,7 @@
                     h, l = turned(h), turned(l)
                 right_s[k, :, (2 * b + e) * cols:(2 * b + e + 1) * cols] = jnp.concatenate(
                     [h, l, h, l], axis=0).astype(jnp.bfloat16)
-        xp = row_j[0, k]
+        xp = col_j[0, k, :, pl.ds(first, rows)]
         hp, lp = split_pair(xp)
         for e in range(2):
             for a in range(2):
@@ -78,7 +79,6 @@
         == lax.broadcasted_iota(jnp.int32, (blocks_c, cols), 1) // blk
     ).astype(jnp.float32)
     wide = dot_nn(flags[0].astype(jnp.float32), spread_c)
-    first = lax.axis_index("stn") * rows
     count = jnp.zeros((blk, cols), jnp.float32)
     for i in range(blocks_r):
         ids = first + i * blk + lax.broadcasted_iota(jnp.int32, (blk, cols), 0)
@@ -200,7 +200,7 @@
     lax.fori_loop(0, dirs // 2, gradient_turn, 0)
 
 
-def device_terms(coherency, vis_data, flags, row_j, col_j):
+def device_terms(coherency, vis_data, flags, col_j):
     chans, dirs, _, rows, cols = coherency.shape
     bf, f4 = jnp.bfloat16, jnp.float32
 
@@ -213,7 +213,7 @@
         jax.ShapeDtypeStruct((chans, dirs * 9, cols), f4),
         jax.ShapeDtypeStruct((chans, 2, 8, cols), f4),
     ]
-    ins = (coherency, vis_data, flags, row_j, col_j)
+    ins = (coherency, vis_data, flags, col_j)
     vm = pltpu.VMEM
     return pl.pallas_call(
         kernel,
@@ -243,52 +243,214 @@
     )(*ins)
 
 
+MESH = pl.DeviceIdType.MESH
+
+
+def meet(axes):
+    barrier = pltpu.get_barrier_semaphore()
+    total = 0
+    for axis, size in axes:
+        me = lax.axis_index(axis)
+        for j in range(1, size):
+            pl.semaphore_signal(
+                barrier, inc=1, device_id={axis: lax.rem(me + j, size)}, device_id_type=MESH)
+            total += 1
+    pl.semaphore_wait(barrier, total)
+
+
+def remote(src, dst, send, recv, axis, target):
+    return pltpu.make_async_remote_copy(
+        src_ref=src, dst_ref=dst, send_sem=send, recv_sem=recv,
+        device_id={axis: target}, device_id_type=MESH)
+
+
+def gather_kernel(
+    stn_count, chan_count, gains, beam, group_of,
+    all_j, factor_out, smooth_out, square_out,
+    before, after, send_sem, recv_sem, side_send, side_recv,
+):
+    chans, dirs, rows = gains.shape[0], gains.shape[4], gains.shape[5]
+    groups = beam.shape[0]
+    me = lax.axis_index("stn")
+    chan = lax.axis_index("chan")
+    barrier = pltpu.get_barrier_semaphore()
+    for j in range(1, stn_count):
+        pl.semaphore_signal(
+            barrier, inc=1, device_id={"stn": lax.rem(me + j, stn_count)}, device_id_type=MESH)
+    up = lax.rem(chan + 1, chan_count)
+    down = lax.rem(chan + chan_count - 1, chan_count)
+    for target in (up, down):
+        pl.semaphore_signal(barrier, inc=1, device_id={"chan": target}, device_id_type=MESH)
+
+    first = pl.multiple_of(me * rows, 128)
+    own_groups = group_of[:, pl.ds(first, rows)]
+    onehot = (
+        jnp.broadcast_to(own_groups, (groups, rows))
+        == lax.broadcasted_iota(jnp.int32, (groups, rows), 0)
+    ).astype(jnp.float32)
+    high, rest = split_pair(beam[...])
+    mid, low = split_pair(rest)
+    factor = dot_tn(high, onehot) + (dot_tn(mid, onehot) + dot_tn(low, onehot))
+    factor_out[...] = factor
+    for f in range(chans):
+        for e in range(2):
+            for x in range(2):
+                for d in range(2):
+                    all_j[f, :, 4 * x + 2 * e + d, pl.ds(first, rows)] = gains[f, e, x, d] * factor
+
+    pl.semaphore_wait(barrier, stn_count + 1)
+    own = all_j.at[:, :, :, pl.ds(first, rows)]
+    copies = [
+        remote(own, own, send_sem.at[j - 1], recv_sem.at[j - 1], "stn", lax.rem(me + j, stn_count))
+        for j in range(1, stn_count)
+    ]
+    sides = [
+        remote(gains.at[pl.ds(chans - 2, 2)], before, side_send.at[0], side_recv.at[0], "chan", up),
+        remote(gains.at[pl.ds(0, 2)], after, side_send.at[1], side_recv.at[1], "chan", down),
+    ]
+    for copy in copies + sides:
+        copy.start()
+    for copy in sides:
+        copy.wait()
+
+    last_chan = chans * chan_count - 2
+    square = jnp.zeros((dirs, rows), jnp.float32)
+    for e in range(2):
+        for x in range(2):
+            for d in range(2):
+                line = (
+                    [before[i, e, x, d] for i in range(2)]
+                    + [gains[i, e, x, d] for i in range(chans)]
+                    + [after[i, e, x, d] for i in range(2)]
+                )
+                second = []
+                for i in range(chans + 2):
+                    place = chan * chans - 1 + i
+                    inside = ((place >= 1) & (place <= last_chan)).astype(jnp.float32)
+                    second.append((line[i + 2] - 2.0 * line[i + 1] + line[i]) * inside)
+                for i in range(chans):
+                    smooth_out[i, e, x, d] = second[i] - 2.0 * second[i + 1] + second[i + 2]
+                    square = square + second[i + 1] * second[i + 1]
+    square_out[...] = jnp.sum(square.reshape(dirs // 8, 8, rows), axis=0)
+    for copy in copies:
+        copy.wait()
+
+
+def finish_kernel(
+    stn_count, chan_count, row_g, col_g, stats, smooth, square, factor,
+    step_out, loss_out,
+    landed, total, own_sums, buf_stn, buf_chan,
+    send_sem, recv_sem, send_stn, recv_stn, send_chan, recv_chan,
+):
+    chans, _, rows = row_g.shape
+    dirs = factor.shape[0]
+    me, chan = lax.axis_index("stn"), lax.axis_index("chan")
+    own_sums[...] = jnp.zeros_like(own_sums)
+    for i in range(2):
+        part = stats[0, i]
+        for f in range(1, chans):
+            part = part + stats[f, i]
+        part = jnp.sum(part, axis=0, keepdims=True)
+        line = part[:, :128]
+        for at in range(128, part.shape[1], 128):
+            line = line + part[:, at:at + 128]
+        own_sums[i:i + 1, :] = line
+    line = jnp.sum(square[...], axis=0, keepdims=True)
+    part = line[:, :128]
+    for at in range(128, line.shape[1], 128):
+        part = part + line[:, at:at + 128]
+    own_sums[2:3, :] = part
+    buf_stn[me] = own_sums[...]
+
+    meet((("stn", stn_count), ("chan", chan_count)))
+    copies = []
+    small = []
+    for j in range(1, stn_count):
+        peer = lax.rem(me + j, stn_count)
+        small.append(remote(own_sums, buf_stn.at[me], send_stn.at[j - 1], recv_stn.at[j - 1], "stn", peer))
+        copies.append(remote(
+            col_g.at[:, :, pl.ds(pl.multiple_of(peer * rows, 128), rows)],
+            landed.at[j - 1], send_sem.at[j - 1], recv_sem.at[j - 1], "stn", peer))
+    for copy in small + copies:
+        copy.start()
+    for copy in small:
+        copy.wait()
+    sums = buf_stn[0]
+    for i in range(1, stn_count):
+        sums = sums + buf_stn[i]
+    own_sums[...] = sums
+    buf_chan[chan] = sums
+    small = [
+        remote(own_sums, buf_chan.at[chan], send_chan.at[j - 1], recv_chan.at[j - 1], "chan",
+               lax.rem(chan + j, chan_count))
+        for j in range(1, chan_count)
+    ]
+    for copy in small:
+        copy.start()
+    for f in range(chans):
+        total[f] = row_g[f] + col_g[f, :, pl.ds(pl.multiple_of(me * rows, 128), rows)]
+    for j, copy in enumerate(copies):
+        copy.wait()
+        for f in range(chans):
+            total[f] = total[f] + landed[j, f]
+    for copy in small:
+        copy.wait()
+    sums = buf_chan[0]
+    for i in range(1, chan_count):
+        sums = sums + buf_chan[i]
+    sums = jnp.sum(sums, axis=1, keepdims=True)
+    scale = (chans * chan_count * rows * stn_count) / sums[0:1]
+    wide = jnp.broadcast_to(scale, (dirs, rows))
+    gain = factor[...]
+    for f in range(chans):
+        curv = wide * gain * gain * total[f, dirs * 8:dirs * 9, :] + damping
+        for e in range(2):
+            for x in range(2):
+                for d in range(2):
+                    grad = total[f, pl.ds(4 * x + 2 * e + d, dirs, stride=8), :]
+                    top = smooth_weight * smooth[f, e, x, d] - wide * gain * grad
+                    step_out[f, e, x, d] = top / curv
+    loss = (scale * sums[1:2] + smooth_weight * sums[2:3]) / (chans * chan_count * rows * stn_count)
+    loss_out[...] = jnp.broadcast_to(loss, loss_out.shape)
+
+
 def on_device(gains, coherency, vis_data, flags, beam, group_of):
     chans, dirs, rows = gains.shape[0], gains.shape[4], gains.shape[5]
-    stn_count = lax.axis_size("stn")
-    chan_count = lax.axis_size("chan")
-    stn_index = lax.axis_index("stn")
-    all_stations = rows * stn_count
-    all_channels = chans * chan_count
-    groups = beam.shape[0]
-    own_groups = lax.dynamic_slice_in_dim(group_of, stn_index * rows, rows, 0)
-    onehot = (own_groups[None, :] == jnp.arange(groups, dtype=jnp.int32)[:, None]).astype(jnp.float32)
-    factor = jnp.sum(beam[:, :, None] * onehot[:, None, :], axis=0)
-
-    own_t = jnp.transpose(gains * factor, (0, 4, 2, 1, 3, 5)).reshape(chans, dirs, 8, rows)
-    all_t = lax.all_gather(own_t, "stn", axis=3, tiled=True)
-
-    ends = chan_count - 1
-    last = gains[chans - 2:]
-    head = gains[:2]
-    before = lax.ppermute(last, "chan", [(i, i + 1) for i in range(ends)])
-    after = lax.ppermute(head, "chan", [(i + 1, i) for i in range(ends)])
-    extended = jnp.concatenate([before, gains, after], axis=0)
-    second = extended[2:] - 2.0 * extended[1:-1] + extended[:-2]
-    first_chan = lax.axis_index("chan") * chans
-    positions = first_chan - 1 + jnp.arange(chans + 2, dtype=jnp.int32)
-    inside = ((positions >= 1) & (positions <= all_channels - 2)).astype(jnp.float32)
-    second = second * inside[:, None, None, None, None, None]
-    smooth_grad = second[:-2] - 2.0 * second[1:-1] + second[2:]
-    own_second = second[1:-1]
-    smooth_local = jnp.sum(own_second * own_second)
-
-    row_out, col_out, stats = device_terms(coherency, vis_data, flags, own_t, all_t)
-    summed = lax.psum_scatter(col_out, "stn", scatter_dimension=2, tiled=True) + row_out
-    local = jnp.stack([jnp.sum(stats[:, 0]), jnp.sum(stats[:, 1]), smooth_local])
-    count_total, sq_total, smooth_total = lax.psum(local, ("chan", "stn"))
-
-    norm_scale = all_channels * all_stations / count_total
-    grad = summed[:, :dirs * 8].reshape(chans, dirs, 2, 2, 2, rows)
-    grad = -jnp.transpose(grad, (0, 3, 2, 4, 1, 5))
-    curv = summed[:, dirs * 8:]
-    gradient = norm_scale * factor * grad + smooth_weight * smooth_grad
-    curvature = norm_scale * factor * factor * curv + damping
-    gain_step = gradient / curvature[:, None, None, None]
-    loss_value = (norm_scale * sq_total + smooth_weight * smooth_total) / (
-        all_channels * all_stations
-    )
-    return (gain_step, loss_value)
+    stn, chan = lax.axis_size("stn"), lax.axis_size("chan")
+    f4 = jnp.float32
+    dma, vm = pltpu.SemaphoreType.DMA, pltpu.VMEM
+    shape = jax.ShapeDtypeStruct
+    all_j, factor, smooth, square = pl.pallas_call(
+        functools.partial(gather_kernel, stn, chan),
+        out_shape=[
+            shape((chans, dirs, 8, rows * stn), f4),
+            shape((dirs, rows), f4),
+            shape(gains.shape, f4),
+            shape((8, rows), f4),
+        ],
+        scratch_shapes=[
+            vm((2,) + gains.shape[1:], f4),
+            vm((2,) + gains.shape[1:], f4),
+            dma((stn - 1,)), dma((stn - 1,)), dma((2,)), dma((2,)),
+        ],
+        compiler_params=pltpu.CompilerParams(collective_id=0, has_side_effects=True),
+    )(gains, beam, group_of.reshape(1, -1))
+    row_g, col_g, stats = device_terms(coherency, vis_data, flags, all_j)
+    gain_step, loss = pl.pallas_call(
+        functools.partial(finish_kernel, stn, chan),
+        out_shape=[shape(gains.shape, f4), shape((8, 128), f4)],
+        scratch_shapes=[
+            vm((stn - 1,) + row_g.shape, f4),
+            vm(row_g.shape, f4),
+            vm((8, 128), f4),
+            vm((stn, 8, 128), f4),
+            vm((chan, 8, 128), f4),
+            dma((stn - 1,)), dma((stn - 1,)), dma((stn - 1,)), dma((stn - 1,)),
+            dma((chan - 1,)), dma((chan - 1,)),
+        ],
+        compiler_params=pltpu.CompilerParams(collective_id=1, has_side_effects=True),
+    )(row_g, col_g, stats, smooth, square, factor)
+    return (gain_step, loss[0, 0])
 
 
 def solution(mesh):

time: 146 us -> 90.5 us (0.62)
  blocking collectives: 50.2 us -> 0 us
  Pallas kernels: 60.5 us -> 85.9 us
  between operations: 17.2 us -> 0.65 us
  other arithmetic: 7.53 us -> 0 us
  starting transfers between devices: 5.88 us -> 0 us
  waiting for transfers between devices: 3.11 us -> 0 us
    psum x1 -> x0, blocking collectives: 41 us -> none  [on_device(): count_total, sq_total, smooth_total = lax.psum(local, ('chan', 'stn'))]
    pallas_call x0 -> x2, Pallas kernels: none -> 25.4 us  [the longest x1 13.7 us: on_device(): pl.pallas_call(functools.partial(gather_kernel, stn, chan), out_shape=[sh...]
    all_gather x1 -> x0, blocking collectives: 9.11 us -> none  [on_device(): all_t = lax.all_gather(own_t, 'stn', axis=3, tiled=True)]
    ppermute x2 -> x0, starting transfers between devices: 5.85 us -> none  [the longest x1 4.55 us: on_device(): before = lax.ppermute(last, 'chan', [(i, i + 1) for i in range(ends)])]
    ppermute x2 -> x0, waiting for transfers between devices: 3.07 us -> none  [the longest x1 2.71 us: on_device(): before = lax.ppermute(last, 'chan', [(i, i + 1) for i in range(ends)])]
    reduce_sum x3 -> x0, other arithmetic: 2.8 us -> none  [the longest x1 1.4 us: on_device(): jnp.sum(stats[:, 0])]
    another operation x1 -> x0, other arithmetic: 1.98 us -> none  [on_device(): jnp.stack([jnp.sum(stats[:, 0]), jnp.sum(stats[:, 1]), smooth_local])]
    unnamed x4 -> x1, local copies, waits for them, and re-layouts: 0.01 us -> 1.57 us
  transfers between devices with their start and end apart: 3 -> 0, of which waited for: 2 -> 0; matrix products, arithmetic and copies ran while one was open for 3% -> 0% of each run, Pallas kernels for 0% -> 0%
where the time goes in v2:
time: 90.5 us; the launch traced here: 89.3 us
  Pallas kernels  85.9 us (95%)
  local copies, waits for them, and re-layouts  2.75 us (3%)
    pallas_call x1, Pallas kernels, device_terms(): pl.pallas_call(kernel, grid=(chans,), in_specs=[per_chan(x.shape) for x i...  60.5 us
    pallas_call x1, Pallas kernels, on_device(): pl.pallas_call(functools.partial(gather_kernel, stn, chan), out_shape=[sh...  13.7 us
    pallas_call x1, Pallas kernels, on_device(): pl.pallas_call(functools.partial(finish_kernel, stn, chan), out_shape=[sh...  11.7 us

profile of v2, /device:TPU:0, one launch (start us, length us, event | category | flops | bytes accessed | tf_op | source)
XLA Modules:
  0.0 89.3 jit_solution(2511423934715381166)
XLA Ops:
  0.6 13.7 %shard_map.77 = (f32[2,16,8,512]{3,2,1,0:T(8,128)}, f32[16,128]{1,0:T(8,128)}, f32[2,2,2,2,16,128]{5,4,3,2,1,0:T(8,128)}, f32[8,128]{1,0:T(8,128)}) custom-call(f32[2,2,2,2,16,128]{5,4,3,2,1,0:T(8,128)} %gains.1, f32[8,16]{1,0:T(8,128)} %beam.1, s32[1,512]{1,0:T(1,128)} %bitcast.2), custom_call_target="tpu_custom_call" | custom-call | tf_op jit(solution)/shard_map/pallas_call | solution.py:423
  14.4 60.5 %shard_map.78 = (f32[2,144,128]{2,1,0:T(8,128)}, f32[2,144,512]{2,1,0:T(8,128)}, f32[2,2,8,512]{3,2,1,0:T(8,128)}) custom-call(bf16[2,16,2,128,512]{4,3,2,1,0:T(8,128)(2,1)} %coh.1, bf16[2,2,2,2,128,512]{5,4,3,2,1,0:T(8,128)(2,1)} %vis.1, s32[2,8,32]{2,1,0:T(8,128)} %flags.1, f32[2,16,8,512]{3,2,1,0:T(8,128)} %get-tuple-element.11.col_j), custom_call_target="tpu_custom_call" | custom-call | tf_op jit(solution)/shard_map/pallas_call | solution.py:218
  74.8 11.7 %shard_map.79 = (f32[2,2,2,2,16,128]{5,4,3,2,1,0:T(8,128)}, f32[8,128]{1,0:T(8,128)}) custom-call(f32[2,144,128]{2,1,0:T(8,128)} %get-tuple-element.12.row_g, f32[2,144,512]{2,1,0:T(8,128)} %get-tuple-element.13.col_g, f32[2,2,8,512]{3,2,1,0:T(8,128)} %get-tuple-element.14.stats, f32[2,2,2,2,16,128]{5,4,3,2,1,0:T(8,128)} %get-tuple-element.15.smooth, ...), custom_call_target="tpu_custom_call" | custom-call | tf_op jit(solution)/shard_map/pallas_call | solution.py:439
  86.5 1.2 %slice.3 = f32[1,1]{1,0:T(1,128)} slice(f32[8,128]{1,0:T(8,128)} %get-tuple-element.19), slice={[0:1], [0:1]} | slice | bytes 8 | tf_op jit(solution)/shard_map/slice | solution.py:453
  87.7 1.6 %copy.9 = f32[2,2,2,2,16,128]{5,4,3,2,1,0:T(8,128)} copy(f32[2,2,2,2,16,128]{5,4,3,2,1,0:T(8,128)} %get-tuple-element.22) | data formatting | bytes 262144

commit v3 on v2

--- a/solution.py
+++ b/solution.py
@@ -411,7 +411,7 @@
                     top = smooth_weight * smooth[f, e, x, d] - wide * gain * grad
                     step_out[f, e, x, d] = top / curv
     loss = (scale * sums[1:2] + smooth_weight * sums[2:3]) / (chans * chan_count * rows * stn_count)
-    loss_out[...] = jnp.broadcast_to(loss, loss_out.shape)
+    loss_out[0, 0] = jnp.sum(loss)
 
 
 def on_device(gains, coherency, vis_data, flags, beam, group_of):
@@ -438,7 +438,11 @@
     row_g, col_g, stats = device_terms(coherency, vis_data, flags, all_j)
     gain_step, loss = pl.pallas_call(
         functools.partial(finish_kernel, stn, chan),
-        out_shape=[shape(gains.shape, f4), shape((8, 128), f4)],
+        out_shape=[shape(gains.shape, f4), shape((1, 1), f4)],
+        out_specs=[
+            pl.BlockSpec(memory_space=pltpu.VMEM),
+            pl.BlockSpec(memory_space=pltpu.SMEM),
+        ],
         scratch_shapes=[
             vm((stn - 1,) + row_g.shape, f4),
             vm(row_g.shape, f4),
@@ -450,7 +454,7 @@
         ],
         compiler_params=pltpu.CompilerParams(collective_id=1, has_side_effects=True),
     )(row_g, col_g, stats, smooth, square, factor)
-    return (gain_step, loss[0, 0])
+    return (gain_step, loss.reshape(()))
 
 
 def solution(mesh):

time: 90.5 us -> 91 us (level)
  between operations: 0.65 us -> 2.32 us
  local copies, waits for them, and re-layouts: 2.75 us -> 1.57 us
    slice x1 -> x0, local copies, waits for them, and re-layouts: 1.19 us -> none  [on_device(): return (gain_step, loss[0, 0])]
where the time goes in v3:
time: 91 us; the launch traced here: 89.8 us
  Pallas kernels  85.9 us (94%)
  between operations  2.32 us (3%)
  local copies, waits for them, and re-layouts  1.57 us (2%)
    pallas_call x1, Pallas kernels, device_terms(): pl.pallas_call(kernel, grid=(chans,), in_specs=[per_chan(x.shape) for x i...  60.5 us
    pallas_call x1, Pallas kernels, on_device(): pl.pallas_call(functools.partial(gather_kernel, stn, chan), out_shape=[sh...  13.7 us
    pallas_call x1, Pallas kernels, on_device(): pl.pallas_call(functools.partial(finish_kernel, stn, chan), out_shape=[sh...  11.7 us

profile of v3, /device:TPU:0, one launch (start us, length us, event | category | flops | bytes accessed | tf_op | source)
XLA Modules:
  0.0 89.8 jit_solution(8238190449531222882)
XLA Ops:
  0.6 13.7 %shard_map.77 = (f32[2,16,8,512]{3,2,1,0:T(8,128)}, f32[16,128]{1,0:T(8,128)}, f32[2,2,2,2,16,128]{5,4,3,2,1,0:T(8,128)}, f32[8,128]{1,0:T(8,128)}) custom-call(f32[2,2,2,2,16,128]{5,4,3,2,1,0:T(8,128)} %gains.1, f32[8,16]{1,0:T(8,128)} %beam.1, s32[1,512]{1,0:T(1,128)} %bitcast.2), custom_call_target="tpu_custom_call" | custom-call | tf_op jit(solution)/shard_map/pallas_call | solution.py:423
  14.4 60.5 %shard_map.78 = (f32[2,144,128]{2,1,0:T(8,128)}, f32[2,144,512]{2,1,0:T(8,128)}, f32[2,2,8,512]{3,2,1,0:T(8,128)}) custom-call(bf16[2,16,2,128,512]{4,3,2,1,0:T(8,128)(2,1)} %coh.1, bf16[2,2,2,2,128,512]{5,4,3,2,1,0:T(8,128)(2,1)} %vis.1, s32[2,8,32]{2,1,0:T(8,128)} %flags.1, f32[2,16,8,512]{3,2,1,0:T(8,128)} %get-tuple-element.11.col_j), custom_call_target="tpu_custom_call" | custom-call | tf_op jit(solution)/shard_map/pallas_call | solution.py:218
  74.8 11.7 %shard_map.79 = (f32[2,2,2,2,16,128]{5,4,3,2,1,0:T(8,128)}, f32[1,1]{1,0:T(1,128)}) custom-call(f32[2,144,128]{2,1,0:T(8,128)} %get-tuple-element.12.row_g, f32[2,144,512]{2,1,0:T(8,128)} %get-tuple-element.13.col_g, f32[2,2,8,512]{3,2,1,0:T(8,128)} %get-tuple-element.14.stats, f32[2,2,2,2,16,128]{5,4,3,2,1,0:T(8,128)} %get-tuple-element.15.smooth, ...), custom_call_target="tpu_custom_call" | custom-call | tf_op jit(solution)/shard_map/pallas_call | solution.py:439
  86.5 1.6 %copy.10 = f32[2,2,2,2,16,128]{5,4,3,2,1,0:T(8,128)} copy(f32[2,2,2,2,16,128]{5,4,3,2,1,0:T(8,128)} %get-tuple-element.22) | data formatting | bytes 262144
